TPU v7x, 32 devices: a whole 2x2x4 slice. The times are simulated.
32 devices in a mesh: mp: 8 (over z, x), seq: 4 (over y, core).
Axes of the slice: x: 2, y: 2, z: 4, core: 2. Of those that a mesh axis runs over, the one named last changes fastest.
Arguments:
- hidden_in: bfloat16 [256, 8192], P(None, 'mp'), may hold values from -4 to 4
- attn_gain: bfloat16 [8192], P('mp'), may hold values from 0.099609375 to 1.8984375
- mlp_gain: bfloat16 [8192], replicated, may hold values from 0.099609375 to 1.8984375
- w_query: bfloat16 [8192, 8192], P('mp', 'seq'), may hold values from -1 to 1
- w_key: bfloat16 [8192, 1024], P('mp', 'seq'), may hold values from -1 to 1
- w_value: bfloat16 [8192, 1024], P('mp', 'seq'), may hold values from -0.0625 to 0.0625
- w_out: bfloat16 [8192, 8192], P('seq', 'mp'), may hold values from -0.0625 to 0.0625
- w_gate: bfloat16 [8192, 28672], P(None, ('mp', 'seq')), may hold values from -0.0625 to 0.0625
- w_up: bfloat16 [8192, 28672], P(None, ('mp', 'seq')), may hold values from -0.0625 to 0.0625
- w_down: bfloat16 [28672, 8192], P(('mp', 'seq')), may hold values from -0.03125 to 0.03125
- prompt_cache: bfloat16 [8, 8, 32768, 256], P(None, 'seq', 'mp'), may hold values from -136 to 136
- tail_cache: bfloat16 [128, 8, 512, 256], P('mp', 'seq'), may hold values from -136 to 136
- prompt_len: int32 [8], replicated, may hold values from 4096 to 32768, as said below
- tail_len: int32 [128], replicated, may hold values from 1 to 512, as said below
- prompt_of: int32 [128], replicated, may hold values from 0 to 7, as said below
Outputs:
- layer_out: bfloat16 [256, 8192], P(('mp', 'seq'))
- input_rms: float32 [256], replicated
- max_logit: float32 [128, 64], P(None, 'seq')
- new_entries: bfloat16 [128, 8, 2, 256], P('mp', 'seq')
Inputs may be any that keep to these rules, and one draw needn't show every extreme that they name: `prompt_len`: at least one prompt has 32768 positions. `tail_len`: at least one request has 512 tail positions. `prompt_of`: each prompt feeds exactly 16 requests.
All inputs are finite; a program needn't handle non-finite values.
Results may differ from a plain program's by a relative error of at most 0.028.
The roundings to bfloat16 on the way count: a program that leaves them out, or rounds other values in their place, can miss the bound.
Values may be sent and summed in bfloat16 or wider, within the bound.
A program may use at most 320 MiB of HBM per device.

v0:
```python
import jax
import jax.numpy as jnp
from jax import lax
from jax.sharding import PartitionSpec as P

D = 8192
HD = 128
PROMPTS = 8
CONT = 16
QPK = 8
REQ = 128


EPS = 1e-05
THETA = 500000.0
NEG = -1e30


def joined(part, axis, combine):
    gathered = jax.tree.map(lambda a: lax.all_gather(a, axis), part)

    def take(source):
        return jax.tree.map(lambda a: lax.dynamic_index_in_dim(a, source, 0, False), gathered)

    return lax.fori_loop(
        1, lax.axis_size(axis), lambda source, state: combine(state, take(source)), take(0)
    )


def rope_table(position, head_dim):
    half_width = head_dim // 2
    frequency = THETA ** (-(jnp.arange(half_width, dtype=jnp.float32) * 2.0 / head_dim))
    rotation = position.astype(jnp.float32)[:, None] * frequency[None, :]
    return (jnp.cos(rotation), jnp.sin(rotation))


def apply_rope(vectors, cosine, sine_table):
    half_width = vectors.shape[-1] // 2
    first_half = vectors[..., :half_width]
    second_half = vectors[..., half_width:]
    cos_rows = cosine[:, None, :]
    sin_rows = sine_table[:, None, :]
    return jnp.concatenate(
        [
            first_half * cos_rows - second_half * sin_rows,
            second_half * cos_rows + first_half * sin_rows,
        ],
        axis=-1,
    )


def merge_partials(earlier, later):
    top_early, total_early, accum_early = earlier
    top_late, total_late, accum_late = later
    highest = jnp.maximum(top_early, top_late)
    factor_early = jnp.exp(top_early - highest)
    factor_late = jnp.exp(top_late - highest)
    return (
        highest,
        total_early * factor_early + total_late * factor_late,
        accum_early * factor_early[..., None] + accum_late * factor_late[..., None],
    )


def softmax_terms(scores, valid_mask):
    masked = jnp.where(valid_mask, scores, NEG)
    highest = jnp.max(masked, axis=-1)
    weights = jnp.where(valid_mask, jnp.exp(masked - highest[..., None]), 0.0)
    return (highest, jnp.sum(weights, axis=-1), weights.astype(jnp.bfloat16))


def prompt_terms(queries, cache_block, lengths, first_place):
    head_dim = queries.shape[-1]
    keys_block = cache_block[..., :head_dim]
    values_block = cache_block[..., head_dim:]
    scores = jnp.einsum(
        "pntgqd,pgjd->pntgqj", queries, keys_block, preferred_element_type=jnp.float32
    ) * head_dim ** (-0.5)
    places = first_place + jnp.arange(cache_block.shape[2], dtype=jnp.int32)
    valid_mask = (places[None, :] < lengths[:, None])[:, None, None, None, None, :]
    highest, totals, weights = softmax_terms(scores, valid_mask)
    accum = jnp.einsum(
        "pntgqj,pgjd->pntgqd", weights, values_block, preferred_element_type=jnp.float32
    )
    return (highest, totals, accum)


def shards(
    hidden_in,
    attn_gain,
    mlp_gain,
    w_query,
    w_key,
    w_value,
    w_out,
    w_gate,
    w_up,
    w_down,
    prompt_cache,
    tail_cache,
    prompt_len,
    tail_len,
    prompt_of,
):
    model_index = lax.axis_index("mp")
    seq_index = lax.axis_index("seq")
    model_count = lax.axis_size("mp")
    seq_count = lax.axis_size("seq")
    row_total = hidden_in.shape[0]
    kv_local = prompt_cache.shape[1]
    local_span = prompt_cache.shape[2]
    head_local = w_query.shape[1] // HD
    req_local = tail_cache.shape[0]
    tail_span = tail_cache.shape[2]
    row_share = row_total // (model_count * seq_count)
    score_scale = HD ** (-0.5)
    wide_in = hidden_in.astype(jnp.float32)
    scaled_in = (wide_in * attn_gain.astype(jnp.float32)[None, :]).astype(jnp.bfloat16)
    query_part = jnp.dot(scaled_in, w_query, preferred_element_type=jnp.float32)
    key_part = jnp.dot(scaled_in, w_key, preferred_element_type=jnp.float32)
    value_part = jnp.dot(scaled_in, w_value, preferred_element_type=jnp.float32)
    square_part = jnp.sum(wide_in * wide_in, axis=1)
    query_sum, key_sum, value_sum, square_sum = lax.psum(
        (query_part, key_part, value_part, square_part), "mp"
    )
    input_rms = jnp.sqrt(square_sum / D)
    inverse_rms = lax.rsqrt(square_sum / D + EPS)
    prompt_match = prompt_of[:, None] == jnp.arange(PROMPTS, dtype=jnp.int32)[None, :]
    prompt_start = jnp.sum(jnp.where(prompt_match, prompt_len[None, :], 0), axis=1)
    position = (
        (prompt_start + tail_len)[:, None] + jnp.arange(2, dtype=jnp.int32)[None, :]
    ).reshape(row_total)
    cosine, sine_table = rope_table(position, HD)
    query = apply_rope(
        (query_sum * inverse_rms[:, None]).reshape(row_total, head_local, HD), cosine, sine_table
    ).astype(jnp.bfloat16)
    key_new = apply_rope(
        (key_sum * inverse_rms[:, None]).reshape(row_total, kv_local, HD), cosine, sine_table
    ).astype(jnp.bfloat16)
    value_new = (
        (value_sum * inverse_rms[:, None]).astype(jnp.bfloat16).reshape(row_total, kv_local, HD)
    )
    row_first = model_index * (2 * req_local)
    own_keys = lax.dynamic_slice_in_dim(key_new, row_first, 2 * req_local, 0)
    own_values = lax.dynamic_slice_in_dim(value_new, row_first, 2 * req_local, 0)
    entries = jnp.concatenate([own_keys, own_values], axis=-1).reshape(
        req_local, 2, kv_local, 2 * HD
    )
    new_entries = jnp.transpose(entries, (0, 2, 1, 3))
    order = jnp.argsort(prompt_of, stable=True)
    inverse_order = jnp.argsort(order)
    query_grid = query.reshape(REQ, 2, kv_local, QPK, HD)
    grouped = query_grid[order].reshape(PROMPTS, CONT, 2, kv_local, QPK, HD)
    first_place = model_index * local_span
    highest, totals, accum = prompt_terms(grouped, prompt_cache, prompt_len, first_place)
    prompt_top = highest.reshape(REQ, 2, head_local)[inverse_order].reshape(row_total, head_local)
    prompt_total = totals.reshape(REQ, 2, head_local)[inverse_order].reshape(row_total, head_local)
    prompt_accum = accum.reshape(REQ, 2, head_local, HD)[inverse_order].reshape(
        row_total, head_local, HD
    )
    own_query = lax.dynamic_slice_in_dim(query_grid, model_index * req_local, req_local, 0)
    own_tail = lax.dynamic_slice_in_dim(tail_len, model_index * req_local, req_local, 0)
    tail_scores = (
        jnp.einsum(
            "ntgqd,ngjd->ntgqj", own_query, tail_cache[..., :HD], preferred_element_type=jnp.float32
        )
        * score_scale
    )
    tail_mask = (jnp.arange(tail_span, dtype=jnp.int32)[None, :] < own_tail[:, None])[
        :, None, None, None, :
    ]
    tail_top, tail_total, tail_weights = softmax_terms(tail_scores, tail_mask)
    tail_accum = jnp.einsum(
        "ntgqj,ngjd->ntgqd", tail_weights, tail_cache[..., HD:], preferred_element_type=jnp.float32
    )
    self_keys = own_keys.reshape(req_local, 2, kv_local, HD)
    self_values = own_values.reshape(req_local, 2, kv_local, HD)
    self_scores = (
        jnp.einsum("ntgqd,nugd->ntgqu", own_query, self_keys, preferred_element_type=jnp.float32)
        * score_scale
    )
    step_mask = (
        jnp.arange(2, dtype=jnp.int32)[None, :] <= jnp.arange(2, dtype=jnp.int32)[:, None]
    )[None, :, None, None, :]
    self_top, self_total, self_weights = softmax_terms(self_scores, step_mask)
    self_accum = jnp.einsum(
        "ntgqu,nugd->ntgqd", self_weights, self_values, preferred_element_type=jnp.float32
    )
    own_top, own_total, own_accum = merge_partials(
        (tail_top, tail_total, tail_accum), (self_top, self_total, self_accum)
    )
    full_top = lax.dynamic_update_slice_in_dim(
        jnp.full((row_total, head_local), NEG, jnp.float32),
        own_top.reshape(2 * req_local, head_local),
        row_first,
        0,
    )
    full_total = lax.dynamic_update_slice_in_dim(
        jnp.zeros((row_total, head_local), jnp.float32),
        own_total.reshape(2 * req_local, head_local),
        row_first,
        0,
    )
    full_accum = lax.dynamic_update_slice_in_dim(
        jnp.zeros((row_total, head_local, HD), jnp.float32),
        own_accum.reshape(2 * req_local, head_local, HD),
        row_first,
        0,
    )
    local_top, local_total, local_accum = merge_partials(
        (prompt_top, prompt_total, prompt_accum), (full_top, full_total, full_accum)
    )
    merged_top, merged_total, merged_accum = joined(
        (local_top, local_total, local_accum), "mp", merge_partials
    )
    attention = (
        (merged_accum / merged_total[..., None])
        .astype(jnp.bfloat16)
        .reshape(row_total, head_local * HD)
    )
    max_logit = jnp.max(merged_top.reshape(REQ, 2, head_local), axis=1)
    head_part = jnp.dot(attention, w_out, preferred_element_type=jnp.float32)
    own_row = (model_index * seq_count + seq_index) * row_share
    head_whole = lax.psum(head_part, "seq")
    residual = (wide_in + head_whole).astype(jnp.bfloat16)
    piece = lax.all_gather(residual, "mp", axis=1, tiled=True)
    wide_piece = piece.astype(jnp.float32)
    gain_piece = mlp_gain.astype(jnp.float32)
    scaled_piece = (wide_piece * gain_piece[None, :]).astype(jnp.bfloat16)
    gate_acc = jnp.dot(scaled_piece, w_gate, preferred_element_type=jnp.float32)
    up_acc = jnp.dot(scaled_piece, w_up, preferred_element_type=jnp.float32)
    square_acc = jnp.sum(wide_piece * wide_piece, axis=1)
    own_piece = lax.dynamic_slice_in_dim(piece, own_row, row_share, 0)
    own_block = own_piece
    gate_acc, up_acc, square_acc, own_block = (gate_acc, up_acc, square_acc, own_block)
    inverse_mid = lax.rsqrt(square_acc / D + EPS)
    gate_value = gate_acc * inverse_mid[:, None]
    up_value = up_acc * inverse_mid[:, None]
    hidden = (jax.nn.silu(gate_value) * up_value).astype(jnp.bfloat16)
    mlp_rows = lax.psum_scatter(
        jnp.dot(hidden, w_down, preferred_element_type=jnp.float32),
        ("mp", "seq"),
        scatter_dimension=0,
        tiled=True,
    )
    layer_out = (own_block.astype(jnp.float32) + mlp_rows).astype(jnp.bfloat16)
    return (layer_out, input_rms, max_logit, new_entries)


def solution(mesh):
    in_specs = (
        P(None, "mp"),
        P("mp"),
        P(),
        P("mp", "seq"),
        P("mp", "seq"),
        P("mp", "seq"),
        P("seq", "mp"),
        P(None, ("mp", "seq")),
        P(None, ("mp", "seq")),
        P(("mp", "seq"), None),
        P(None, "seq", "mp", None),
        P("mp", "seq", None, None),
        P(),
        P(),
        P(),
    )
    out_specs = (P(("mp", "seq"), None), P(), P(None, "seq"), P("mp", "seq", None, None))
    return jax.shard_map(shards, mesh=mesh, in_specs=in_specs, out_specs=out_specs, check_vma=False)
```

profile of v0, /device:TPU:0, one launch (start us, length us, event | category | flops | bytes accessed | tf_op | source)
XLA Modules:
  0.0 820.9 jit_solution(7491996693346277574)
XLA Ops:
  8.0 4.9 fusion.84
  20.8 24.3 %psum.36 = f32[256]{0:T(256)S(1)} all-reduce(f32[256]{0:T(256)S(1)} %fusion.68), channel_id=1, replica_groups=mesh['mp'=8,'seq'=4] {'mp'}, use_global_device_ids=true, to_apply=%region_2.0 | all-reduce | flops 256 | bytes 2048 | tf_op jit(solution)/shard_map/psum | solution.py:123
  46.4 88.4 %all-reduce.6.cloned.1.call-done = (f32[256,2048]{1,0:T(8,128)}, f32[256,256]{1,0:T(8,128)}, f32[256,256]{1,0:T(8,128)}) async-done(((f32[256,2048]{1,0:T(8,128)}, f32[256,256]{1,0:T(8,128)}, f32[256,256]{1,0:T(8,128)}), (f32[256,2048]{1,0:T(8,128)}, f32[256,256]{1,0:T(8,128)}, f32[256,256]{1,0:T(8,128)})) %all-reduce.6.cloned.1.call-update) | async-done | bytes 2621456 | tf_op jit(solution)/shard_map/psum | solution.py:123
  144.9 29.6 %bitcast_reduce_fusion = (f32[8,16,2,2,8]{4,2,1,3,0:T(2,128)S(1)}, f32[8,2,16,2,8,4096]{5,4,3,2,1,0:T(8,128)}) fusion(pred[8,4096]{1,0:T(8,128)(4,1)S(1)} %broadcast_compare_fusion, bf16[8,2,4096,256]{3,2,1,0:T(8,128)(2,1)} %param.27, bf16[8,16,2,2,8,128]{5,4,2,3,1,0:T(8,128)(2,1)} %bitcast.142), kind=kOutput, calls=%fused_computation.13 | convolution fusion | flops 4345294848 | bytes 84983808 | tf_op jit(solution)/shard_map/pntgqd,pgjd->pntgqj/dot_general | solution.py:76
  174.6 22.1 %fusion.6 = f32[8,16,2,2,8]{4,2,1,3,0:T(2,128)S(1)} fusion(f32[8,2,16,2,8,4096]{5,4,3,2,1,0:T(8,128)} %get-tuple-element.268, f32[8,16,2,2,8]{4,2,1,3,0:T(2,128)S(1)} %get-tuple-element.267, pred[8,4096]{1,0:T(8,128)(4,1)S(1)} %broadcast_compare_fusion), kind=kLoop, calls=%fused_computation.18 | loop fusion | flops 83881984 | bytes 67174400 | tf_op jit(solution)/shard_map/reduce_sum | solution.py:69
  196.8 30.3 %fusion.29 = f32[8,16,2,2,8,128]{5,4,2,1,3,0:T(8,128)} fusion(bf16[8,2,4096,256]{3,2,1,0:T(8,128)(2,1)} %param.27, f32[8,2,16,2,8,4096]{5,4,3,2,1,0:T(8,128)} %get-tuple-element.268, f32[8,16,2,2,8]{4,2,1,3,0:T(2,128)S(1)} %get-tuple-element.267, pred[8,4096]{1,0:T(8,128)(4,1)S(1)} %broadcast_compare_fusion), kind=kOutput, calls=%fused_computation.45 | convolution fusion | flops 4378853376 | bytes 86310912 | tf_op jit(solution)/shard_map/pntgqj,pgjd->pntgqd/dot_general | solution.py:82
  242.2 35.5 %all-gather = f32[2048,16]{1,0:T(8,128)S(1)} all-gather(f32[256,16]{1,0:T(8,128)S(1)} %get-tuple-element.246), channel_id=2, replica_groups=mesh['mp'=8,'seq'=4] {'mp'}, dimensions={0}, use_global_device_ids=true | all-gather | bytes 147456 | tf_op jit(solution)/shard_map/all_gather | solution.py:20
  277.8 36.9 %all-gather.1 = f32[2048,16]{1,0:T(8,128)S(1)} all-gather(f32[256,16]{1,0:T(8,128)S(1)} %get-tuple-element.243), channel_id=3, replica_groups=mesh['mp'=8,'seq'=4] {'mp'}, dimensions={0}, use_global_device_ids=true | all-gather | bytes 147456 | tf_op jit(solution)/shard_map/all_gather | solution.py:20
  315.4 169.5 %all-gather.8.cloned.1.call-done = f32[2048,16,128]{2,1,0:T(8,128)} async-done(((f32[256,16,128]{2,1,0:T(8,128)}), f32[2048,16,128]{2,1,0:T(8,128)}) %all-gather.8.cloned.1.call-update) | async-done | bytes 16777232 | tf_op jit(solution)/shard_map/all_gather | solution.py:20
  486.7 28.6 %while.19 = (s32[]{:T(128)}, f32[256,16]{0,1:T(8,128)S(1)}, f32[256,16]{0,1:T(8,128)S(1)}, f32[256,16,128]{2,1,0:T(8,128)S(1)}, f32[8,256,16]{1,2,0:T(8,128)S(1)...) while((s32[]{:T(128)}, f32[256,16]{0,1:T(8,128)S(1)}, ...), condition=%wide.region_15.16_spmd, body=%wide.region_14.15_spmd.sunk | while | flops 1597445 | bytes 6520983 | solution.py:25
  486.9 3.8 fusion.120
  491.0 3.8 fusion.120
  495.1 3.8 fusion.120
  499.2 3.8 fusion.120
  503.3 3.8 fusion.120
  507.4 3.8 fusion.120
  511.5 3.8 fusion.120
  516.2 4.5 fusion.70
  520.7 34.4 %all-reduce.4.cloned.1.call-done = f32[256,1024]{1,0:T(8,128)} async-done(((f32[256,1024]{1,0:T(8,128)}), f32[256,1024]{1,0:T(8,128)}) %all-reduce.4.cloned.1.call-update) | async-done | bytes 1048592 | tf_op jit(solution)/shard_map/psum | solution.py:224
  557.4 73.8 %all-gather.6.cloned.1.call-done = bf16[256,8192]{1,0:T(8,128)(2,1)} async-done(((bf16[256,1024]{1,0:T(8,128)(2,1)}), bf16[256,8192]{1,0:T(8,128)(2,1)}) %all-gather.6.cloned.1.call-update) | async-done | bytes 4194320 | tf_op jit(solution)/shard_map/all_gather | solution.py:226
  631.2 3.3 fusion.17
  634.7 8.1 fusion.43
  642.8 22.7 %fusion.87 = f32[256,8192]{1,0:T(8,128)} fusion(bf16[896,8192]{1,0:T(8,128)(2,1)} %param.26, bf16[8192,896]{1,0:T(8,128)(2,1)} %param.25, bf16[256,8192]{1,0:T(8,128)(2,1)} %all-gather.6.cloned.1.call-done, f32[8192]{0:T(1024)S(1)} %convert_element_type.71, f32[256,896]{1,0:T(8,128)S(1)} %fusion.43, f32[256]{0:T(256)S(1)} %add_rsqrt_fusion), kind=kOutput, calls=%fused_computation.81 | convolution fusion | flops 7524089856 | bytes 42894336 | tf_op jit(solution)/shard_map/dot_general | solution.py:241
  667.9 144.8 %reduce-scatter.2.cloned.1.call-done = f32[8,8192]{1,0:T(8,128)} async-done(((f32[256,8192]{1,0:T(8,128)}), f32[8,8192]{1,0:T(8,128)}) %reduce-scatter.2.cloned.1.call-update) | async-done | bytes 262160 | tf_op jit(solution)/shard_map/reduce_scatter | solution.py:240
  (155 shorter events, 46.4 us)
Async XLA Ops:
  7.2 5.8 copy-start
  7.2 5.8 copy-start.2
  7.2 6.8 copy-start.6
  7.2 127.7 %all-reduce.6.cloned.1.call-start = ((), (), s32[]{:S(2)}) async-start(), calls=%async_computation.5 | async-start | bytes 5242880 | tf_op jit(solution)/shard_map/psum | solution.py:123
  12.9 2.2 copy-start.12
  13.0 2.2 copy-start.14
  13.0 2.3 copy-start.13
  15.1 469.9 %all-gather.8.cloned.1.call-start = ((), (), s32[]{:S(2)}) async-start(), calls=%async_computation.4 | async-start | bytes 18874368 | tf_op jit(solution)/shard_map/all_gather | solution.py:20
  138.3 2.9 slice-start
  138.7 3.2 slice-start.1
  140.4 0.7 copy-start.7
  227.1 3.9 copy-start.9
  242.2 312.9 %all-reduce.4.cloned.1.call-start = ((), (), s32[]{:S(2)}) async-start(), calls=%async_computation.1 | async-start | bytes 2097152 | tf_op jit(solution)/shard_map/psum | solution.py:224
  515.3 5.3 copy-start.4
  516.2 41.2 %copy-start.11 = (bf16[8192]{0:T(1024)(128)(2,1)S(1)}, bf16[8192]{0:T(1024)(128)(2,1)}, u32[]{:S(2)}) copy-start(bf16[8192]{0:T(1024)(128)(2,1)} %param.19) | copy-start | bytes 49156
  520.7 110.6 %all-gather.6.cloned.1.call-start = ((), (), s32[]{:S(2)}) async-start(), calls=%async_computation.2 | async-start | bytes 4718592 | tf_op jit(solution)/shard_map/all_gather | solution.py:226
  557.3 255.4 %reduce-scatter.2.cloned.1.call-start = ((), (), s32[]{:S(2)}) async-start(), calls=%async_computation.3 | async-start | bytes 8650752 | tf_op jit(solution)/shard_map/reduce_scatter | solution.py:240
  631.2 3.4 copy-start.3
  665.5 148.9 %copy-start.1 = (bf16[1024,256]{1,0:T(8,128)(2,1)S(1)}, bf16[1024,256]{1,0:T(8,128)(2,1)}, u32[]{:S(2)}) copy-start(bf16[1024,256]{1,0:T(8,128)(2,1)} %param.22) | copy-start | bytes 1572868
  665.5 0.8 copy-start.8
  665.5 0.8 copy-start.10
  665.5 1.5 copy-start.5
Sparse Core Ops, SparseCore 0:
  15.2 119.6 all-reduce.5
  242.3 242.5 all-gather.7
  520.8 34.2 all-reduce.3
  557.5 73.7 all-gather.5
  665.6 147.0 reduce-scatter.1
where the time goes:
time: 822 us; the launch traced here: 821 us
  waiting for transfers between devices  511 us (62%)
  matrix products  107 us (13%)
  blocking collectives  96.7 us (12%)
  other arithmetic  72.6 us (9%)
  local copies, waits for them, and re-layouts  18.4 us (2%)
  between operations  14.3 us (2%)
    all_gather x1, waiting for transfers between devices, joined(): gathered = jax.tree.map(lambda a: lax.all_gather(a, axis), part)  169 us
    reduce_scatter x1, waiting for transfers between devices, shards(): lax.psum_scatter(jnp.dot(hidden, w_down, preferred_element_type=jnp.float...  145 us
    psum x1, waiting for transfers between devices, shards(): lax.psum((query_part, key_part, value_part, square_part), 'mp')  88.4 us
    all_gather x1, waiting for transfers between devices, shards(): piece = lax.all_gather(residual, 'mp', axis=1, tiled=True)  73.8 us
    all_gather x2, blocking collectives, joined(): gathered = jax.tree.map(lambda a: lax.all_gather(a, axis), part)  72.5 us
    psum x1, waiting for transfers between devices, shards(): head_whole = lax.psum(head_part, 'seq')  34.4 us
    dot_general x1, matrix products, prompt_terms(): jnp.einsum('pntgqj,pgjd->pntgqd', weights, values_block, preferred_elemen...  30.3 us
    add x8, other arithmetic, merge_partials(): accum_early * factor_early[..., None] + accum_late * factor_late[..., None]  29.7 us
  transfers between devices with their start and end apart: 5, of which 5 were waited for; matrix products, arithmetic and copies ran while one was open for 1% of the time, Pallas kernels for 0%

commit v1 on v0

v1 whole, which is shorter than its diff:
```python
import functools

import jax
import jax.numpy as jnp
from jax import lax
from jax.experimental import pallas as pl
from jax.experimental.pallas import tpu as pltpu
from jax.sharding import PartitionSpec as P

D = 8192
HD = 128
PROMPTS = 8
CONT = 16
QPK = 8
REQ = 128


EPS = 1e-05
THETA = 500000.0
NEG = -1e30
FLOOR = -1e29
MESH = pl.DeviceIdType.MESH


def rope_table(position, head_dim):
    half_width = head_dim // 2
    frequency = THETA ** (-(jnp.arange(half_width, dtype=jnp.float32) * 2.0 / head_dim))
    rotation = position.astype(jnp.float32)[:, None] * frequency[None, :]
    return (jnp.cos(rotation), jnp.sin(rotation))


def apply_rope(vectors, cosine, sine_table):
    half_width = vectors.shape[-1] // 2
    first_half = vectors[..., :half_width]
    second_half = vectors[..., half_width:]
    cos_rows = cosine[:, None, :]
    sin_rows = sine_table[:, None, :]
    return jnp.concatenate(
        [
            first_half * cos_rows - second_half * sin_rows,
            second_half * cos_rows + first_half * sin_rows,
        ],
        axis=-1,
    )


def merge_partials(earlier, later):
    top_early, total_early, accum_early = earlier
    top_late, total_late, accum_late = later
    highest = jnp.maximum(top_early, top_late)
    factor_early = jnp.exp(top_early - highest)
    factor_late = jnp.exp(top_late - highest)
    return (
        highest,
        total_early * factor_early + total_late * factor_late,
        accum_early * factor_early[..., None] + accum_late * factor_late[..., None],
    )


def softmax_terms(scores, valid_mask):
    masked = jnp.where(valid_mask, scores, NEG)
    highest = jnp.max(masked, axis=-1)
    weights = jnp.where(valid_mask, jnp.exp(masked - highest[..., None]), 0.0)
    return (highest, jnp.sum(weights, axis=-1), weights.astype(jnp.bfloat16))


def exchange_kernel(kinds, axis, stride, count, *refs):
    total = len(kinds)
    sources, targets = refs[:total], refs[total : 2 * total]
    send_sem, recv_sem, own_sem = refs[2 * total :]
    me = lax.axis_index(axis)
    place = lax.rem(lax.div(me, stride), count)
    base = me - place * stride
    barrier = pltpu.get_barrier_semaphore()
    for step in range(1, count):
        peer = base + lax.rem(place + step, count) * stride
        pl.semaphore_signal(barrier, inc=1, device_id={axis: peer}, device_id_type=MESH)
    pl.semaphore_wait(barrier, count - 1)
    copies = []
    for step in range(1, count):
        other = lax.rem(place + step, count)
        peer = base + other * stride
        for a in range(total):
            copy = pltpu.make_async_remote_copy(
                src_ref=sources[a].at[other] if kinds[a] == "scatter" else sources[a],
                dst_ref=targets[a].at[place],
                send_sem=send_sem.at[a, step],
                recv_sem=recv_sem.at[a, step],
                device_id={axis: peer},
                device_id_type=MESH,
            )
            copy.start()
            copies.append(copy)
    own = []
    for a in range(total):
        copy = pltpu.make_async_copy(
            sources[a].at[place] if kinds[a] == "scatter" else sources[a],
            targets[a].at[place],
            own_sem.at[a],
        )
        copy.start()
        own.append(copy)
    for copy in own + copies:
        copy.wait()


def exchange(arrays, kinds, axis, stride, count, identity):
    total = len(arrays)
    return pl.pallas_call(
        functools.partial(exchange_kernel, kinds, axis, stride, count),
        out_shape=[
            jax.ShapeDtypeStruct(a.shape if k == "scatter" else (count,) + a.shape, a.dtype)
            for a, k in zip(arrays, kinds)
        ],
        in_specs=[pl.BlockSpec(memory_space=pl.ANY)] * total,
        out_specs=[pl.BlockSpec(memory_space=pl.ANY)] * total,
        scratch_shapes=[
            pltpu.SemaphoreType.DMA((total, count)),
            pltpu.SemaphoreType.DMA((total, count)),
            pltpu.SemaphoreType.DMA((total,)),
        ],
        compiler_params=pltpu.CompilerParams(collective_id=identity, has_side_effects=True),
    )(*arrays)


def prompt_kernel(piece, length_ref, query_ref, cache_ref, accum_ref, stats_ref):
    length = length_ref[pl.program_id(0)]
    queries = query_ref[0, 0]
    rows = queries.shape[0]
    span = cache_ref.shape[2]
    top = jnp.full((rows, 1), FLOOR, jnp.float32)
    total = jnp.zeros((rows, 1), jnp.float32)
    accum = jnp.zeros((rows, HD), jnp.float32)
    for first in range(0, span, piece):
        keys = cache_ref[0, 0, first : first + piece, :HD]
        values = cache_ref[0, 0, first : first + piece, HD:]
        scores = lax.dot_general(
            queries, keys, (((1,), (1,)), ((), ())), preferred_element_type=jnp.float32
        ) * HD ** (-0.5)
        places = first + lax.broadcasted_iota(jnp.int32, (1, piece), 1)
        scores = jnp.where(places < length, scores, NEG)
        highest = jnp.maximum(top, jnp.max(scores, axis=1, keepdims=True))
        factor = jnp.exp(top - highest)
        weights = jnp.exp(scores - highest)
        total = total * factor + jnp.sum(weights, axis=1, keepdims=True)
        accum = accum * factor + jnp.dot(
            weights.astype(jnp.bfloat16), values, preferred_element_type=jnp.float32
        )
        top = highest
    accum_ref[0, 0] = accum.astype(jnp.bfloat16)
    lanes = lax.broadcasted_iota(jnp.int32, (rows, HD), 1)
    stats_ref[0, 0] = jnp.where(lanes < HD // 2, top, total)


def prompt_terms(queries, cache, lengths):
    prompts, heads, rows, _ = queries.shape
    span = cache.shape[2]
    piece = min(span, 1024)

    def place(p, g, lengths):
        return (p, g, 0, 0)

    return pl.pallas_call(
        functools.partial(prompt_kernel, piece),
        out_shape=[
            jax.ShapeDtypeStruct((prompts, heads, rows, HD), jnp.bfloat16),
            jax.ShapeDtypeStruct((prompts, heads, rows, HD), jnp.float32),
        ],
        grid_spec=pltpu.PrefetchScalarGridSpec(
            num_scalar_prefetch=1,
            grid=(prompts, heads),
            in_specs=[
                pl.BlockSpec((1, 1, rows, HD), place),
                pl.BlockSpec((1, 1, span, 2 * HD), place),
            ],
            out_specs=[
                pl.BlockSpec((1, 1, rows, HD), place),
                pl.BlockSpec((1, 1, rows, HD), place),
            ],
        ),
        compiler_params=pltpu.CompilerParams(vmem_limit_bytes=40 * 1024 * 1024),
        cost_estimate=pl.CostEstimate(
            flops=4 * prompts * heads * rows * span * HD,
            bytes_accessed=prompts * heads * span * HD * 4,
            transcendentals=prompts * heads * rows * span,
        ),
    )(lengths, queries, cache)


def shards(
    hidden_in,
    attn_gain,
    mlp_gain,
    w_query,
    w_key,
    w_value,
    w_out,
    w_gate,
    w_up,
    w_down,
    prompt_cache,
    tail_cache,
    prompt_len,
    tail_len,
    prompt_of,
):
    model_index = lax.axis_index("mp")
    seq_index = lax.axis_index("seq")
    model_count = lax.axis_size("mp")
    seq_count = lax.axis_size("seq")
    row_total = hidden_in.shape[0]
    kv_local = prompt_cache.shape[1]
    local_span = prompt_cache.shape[2]
    head_local = w_query.shape[1] // HD
    req_local = tail_cache.shape[0]
    tail_span = tail_cache.shape[2]
    row_share = row_total // (model_count * seq_count)
    score_scale = HD ** (-0.5)
    wide_in = hidden_in.astype(jnp.float32)
    scaled_in = (wide_in * attn_gain.astype(jnp.float32)[None, :]).astype(jnp.bfloat16)
    query_part = jnp.dot(scaled_in, w_query, preferred_element_type=jnp.float32)
    key_part = jnp.dot(scaled_in, w_key, preferred_element_type=jnp.float32)
    value_part = jnp.dot(scaled_in, w_value, preferred_element_type=jnp.float32)
    square_part = jnp.sum(wide_in * wide_in, axis=1)
    own_rows = row_total // model_count
    head_width = head_local * HD
    kv_width = kv_local * HD
    parts = jnp.concatenate([query_part, key_part, value_part], axis=1).astype(jnp.bfloat16)
    square_lanes = jnp.pad(square_part.reshape(row_total // HD, HD), ((0, 8 - row_total // HD), (0, 0)))
    part_all, square_all = exchange(
        [parts.reshape(model_count, own_rows, -1), square_lanes],
        ("scatter", "gather"), "mp", 1, model_count, 1,
    )
    sums = jnp.sum(part_all.astype(jnp.float32), axis=0)
    square_sum = jnp.sum(square_all, axis=0)[: row_total // HD].reshape(row_total)
    input_rms = jnp.sqrt(square_sum / D)
    inverse_rms = lax.rsqrt(square_sum / D + EPS)
    row_first = model_index * own_rows
    prompt_match = prompt_of[:, None] == jnp.arange(PROMPTS, dtype=jnp.int32)[None, :]
    prompt_start = jnp.sum(jnp.where(prompt_match, prompt_len[None, :], 0), axis=1)
    position = (
        (prompt_start + tail_len)[:, None] + jnp.arange(2, dtype=jnp.int32)[None, :]
    ).reshape(row_total)
    own_position = lax.dynamic_slice_in_dim(position, row_first, own_rows, 0)
    cosine, sine_table = rope_table(own_position, HD)
    sums = sums * lax.dynamic_slice_in_dim(inverse_rms, row_first, own_rows, 0)[:, None]
    query_rows = apply_rope(
        sums[:, :head_width].reshape(own_rows, head_local, HD), cosine, sine_table
    ).astype(jnp.bfloat16)
    own_keys = apply_rope(
        sums[:, head_width : head_width + kv_width].reshape(own_rows, kv_local, HD), cosine, sine_table
    ).astype(jnp.bfloat16)
    own_values = sums[:, head_width + kv_width :].astype(jnp.bfloat16).reshape(own_rows, kv_local, HD)
    entries = jnp.concatenate([own_keys, own_values], axis=-1).reshape(
        req_local, 2, kv_local, 2 * HD
    )
    new_entries = jnp.transpose(entries, (0, 2, 1, 3))
    (query_all,) = exchange(
        [query_rows.reshape(own_rows, head_width)], ("gather",), "mp", 1, model_count, 2
    )
    query = query_all.reshape(row_total, head_width)
    requests = jnp.arange(REQ, dtype=jnp.int32)
    ahead = (prompt_of[None, :] < prompt_of[:, None]) | (
        (prompt_of[None, :] == prompt_of[:, None]) & (requests[None, :] < requests[:, None])
    )
    rank = jnp.sum(ahead.astype(jnp.int32), axis=1)
    token_rank = (2 * rank[:, None] + jnp.arange(2, dtype=jnp.int32)[None, :]).reshape(row_total)
    moves = jnp.arange(row_total, dtype=jnp.int32)[:, None] == token_rank[None, :]
    moves_low = moves.astype(jnp.bfloat16)
    grouped = jnp.dot(moves_low, query, preferred_element_type=jnp.float32).astype(jnp.bfloat16)
    grouped = jnp.transpose(
        grouped.reshape(PROMPTS, CONT * 2, kv_local, QPK, HD), (0, 2, 1, 3, 4)
    ).reshape(PROMPTS, kv_local, CONT * 2 * QPK, HD)
    lengths = jnp.clip(prompt_len - model_index * local_span, 0, local_span)
    accum, stats = prompt_terms(grouped, prompt_cache, lengths)

    def token_rows(values):
        width = values.shape[-1]
        values = values.reshape(PROMPTS, kv_local, CONT * 2, QPK, width)
        return jnp.transpose(values, (0, 2, 1, 3, 4)).reshape(row_total, head_local * width)

    back = (((0,), (0,)), ((), ()))
    prompt_accum = lax.dot_general(
        moves_low, token_rows(accum), back, preferred_element_type=jnp.float32
    ).astype(jnp.bfloat16)
    stat_rows = jnp.concatenate(
        [token_rows(stats[..., :1]), token_rows(stats[..., HD // 2 : HD // 2 + 1])], axis=1
    )
    stat_rows = lax.dot_general(
        moves.astype(jnp.float32), stat_rows, back, precision=lax.Precision.HIGHEST,
        preferred_element_type=jnp.float32,
    )
    stat_rows = jnp.pad(stat_rows, ((0, 0), (0, HD - 2 * head_local)))
    accum_all, stat_all = exchange(
        [
            prompt_accum.reshape(model_count, own_rows, head_width),
            stat_rows.reshape(model_count, own_rows, HD),
        ],
        ("scatter", "scatter"), "mp", 1, model_count, 3,
    )
    own_query = query_rows.reshape(req_local, 2, kv_local, QPK, HD)
    own_tail = lax.dynamic_slice_in_dim(tail_len, model_index * req_local, req_local, 0)
    tail_scores = (
        jnp.einsum(
            "ntgqd,ngjd->ntgqj", own_query, tail_cache[..., :HD], preferred_element_type=jnp.float32
        )
        * score_scale
    )
    tail_mask = (jnp.arange(tail_span, dtype=jnp.int32)[None, :] < own_tail[:, None])[
        :, None, None, None, :
    ]
    tail_top, tail_total, tail_weights = softmax_terms(tail_scores, tail_mask)
    tail_accum = jnp.einsum(
        "ntgqj,ngjd->ntgqd", tail_weights, tail_cache[..., HD:], preferred_element_type=jnp.float32
    )
    self_keys = own_keys.reshape(req_local, 2, kv_local, HD)
    self_values = own_values.reshape(req_local, 2, kv_local, HD)
    self_scores = (
        jnp.einsum("ntgqd,nugd->ntgqu", own_query, self_keys, preferred_element_type=jnp.float32)
        * score_scale
    )
    step_mask = (
        jnp.arange(2, dtype=jnp.int32)[None, :] <= jnp.arange(2, dtype=jnp.int32)[:, None]
    )[None, :, None, None, :]
    self_top, self_total, self_weights = softmax_terms(self_scores, step_mask)
    self_accum = jnp.einsum(
        "ntgqu,nugd->ntgqd", self_weights, self_values, preferred_element_type=jnp.float32
    )
    own_top, own_total, own_accum = merge_partials(
        (tail_top, tail_total, tail_accum), (self_top, self_total, self_accum)
    )
    own_top = own_top.reshape(own_rows, head_local)
    own_total = own_total.reshape(own_rows, head_local)
    own_accum = own_accum.reshape(own_rows, head_local, HD)
    tops = stat_all[:, :, :head_local]
    totals = stat_all[:, :, head_local : 2 * head_local]
    merged_top = jnp.maximum(own_top, jnp.max(tops, axis=0))
    factors = jnp.exp(tops - merged_top[None])
    own_factor = jnp.exp(own_top - merged_top)
    merged_total = own_total * own_factor + jnp.sum(totals * factors, axis=0)
    merged_accum = own_accum * own_factor[..., None] + jnp.sum(
        accum_all.reshape(model_count, own_rows, head_local, HD).astype(jnp.float32)
        * factors[..., None],
        axis=0,
    )
    attention_rows = (
        (merged_accum / merged_total[..., None]).astype(jnp.bfloat16).reshape(own_rows, head_width)
    )
    own_max = jnp.max(merged_top.reshape(req_local, 2, head_local), axis=1)
    own_max = jnp.pad(own_max, ((0, 0), (0, HD - head_local)))
    attention_all, max_all = exchange(
        [attention_rows, own_max], ("gather", "gather"), "mp", 1, model_count, 4
    )
    attention = attention_all.reshape(row_total, head_width)
    max_logit = max_all.reshape(REQ, HD)[:, :head_local]
    head_part = jnp.dot(attention, w_out, preferred_element_type=jnp.float32)
    own_row = (model_index * seq_count + seq_index) * row_share
    seq_rows = row_total // seq_count
    cores, chips = 2, seq_count // 2
    (head_all,) = exchange(
        [head_part.reshape(seq_count, seq_rows, -1)], ("scatter",), "seq", 1, seq_count, 5
    )
    wide_rows = lax.dynamic_slice_in_dim(wide_in, seq_index * seq_rows, seq_rows, 0)
    residual = (wide_rows + jnp.sum(head_all, axis=0)).astype(jnp.bfloat16)
    (piece_model,) = exchange([residual], ("gather",), "mp", 1, model_count, 6)
    (piece_chip,) = exchange([piece_model], ("gather",), "seq", cores, chips, 7)
    (piece_core,) = exchange([piece_chip], ("gather",), "seq", 1, cores, 8)
    piece = jnp.transpose(piece_core, (1, 0, 3, 2, 4)).reshape(row_total, -1)
    wide_piece = piece.astype(jnp.float32)
    gain_piece = mlp_gain.astype(jnp.float32)
    scaled_piece = (wide_piece * gain_piece[None, :]).astype(jnp.bfloat16)
    gate_acc = jnp.dot(scaled_piece, w_gate, preferred_element_type=jnp.float32)
    up_acc = jnp.dot(scaled_piece, w_up, preferred_element_type=jnp.float32)
    square_acc = jnp.sum(wide_piece * wide_piece, axis=1)
    own_piece = lax.dynamic_slice_in_dim(piece, own_row, row_share, 0)
    own_block = own_piece
    gate_acc, up_acc, square_acc, own_block = (gate_acc, up_acc, square_acc, own_block)
    inverse_mid = lax.rsqrt(square_acc / D + EPS)
    gate_value = gate_acc * inverse_mid[:, None]
    up_value = up_acc * inverse_mid[:, None]
    hidden = (jax.nn.silu(gate_value) * up_value).astype(jnp.bfloat16)
    down = jnp.dot(hidden, w_down, preferred_element_type=jnp.float32).astype(jnp.bfloat16)
    down = jnp.transpose(
        down.reshape(model_count, chips, cores, row_share, D), (2, 1, 0, 3, 4)
    )
    (down_core,) = exchange(
        [down.reshape(cores, chips * model_count * row_share, D)], ("scatter",), "seq", 1, cores, 9
    )
    down = jnp.sum(down_core.astype(jnp.float32), axis=0).astype(jnp.bfloat16)
    (down_chip,) = exchange(
        [down.reshape(chips, model_count * row_share, D)], ("scatter",), "seq", cores, chips, 10
    )
    down = jnp.sum(down_chip.astype(jnp.float32), axis=0).astype(jnp.bfloat16)
    (down_model,) = exchange(
        [down.reshape(model_count, row_share * 8, D // 8)], ("scatter",), "mp", 1, model_count, 11
    )
    mlp_rows = jnp.sum(down_model.astype(jnp.float32), axis=0).reshape(row_share, D)
    layer_out = (own_block.astype(jnp.float32) + mlp_rows).astype(jnp.bfloat16)
    return (layer_out, input_rms, max_logit, new_entries)


def solution(mesh):
    in_specs = (
        P(None, "mp"),
        P("mp"),
        P(),
        P("mp", "seq"),
        P("mp", "seq"),
        P("mp", "seq"),
        P("seq", "mp"),
        P(None, ("mp", "seq")),
        P(None, ("mp", "seq")),
        P(("mp", "seq"), None),
        P(None, "seq", "mp", None),
        P("mp", "seq", None, None),
        P(),
        P(),
        P(),
    )
    out_specs = (P(("mp", "seq"), None), P(), P(None, "seq"), P("mp", "seq", None, None))
    return jax.shard_map(shards, mesh=mesh, in_specs=in_specs, out_specs=out_specs, check_vma=False)
```

time: 822 us -> 541 us (0.66)
  the two profiles are of different devices: /device:TPU:0 before, /device:TPU:10 now
where the time goes in v1:
time: 541 us; the launch traced here: 535 us
  Pallas kernels  418 us (77%)
  matrix products  48.1 us (9%)
  local copies, waits for them, and re-layouts  34.2 us (6%)
  other arithmetic  33 us (6%)
    pallas_call x11, Pallas kernels, exchange(): pl.pallas_call(functools.partial(exchange_kernel, kinds, axis, stride, co...  382 us
    pallas_call x1, Pallas kernels, prompt_terms(): pl.pallas_call(functools.partial(prompt_kernel, piece), out_shape=[jax.Sh...  35.6 us

profile of v1, /device:TPU:10, one launch (start us, length us, event | category | flops | bytes accessed | tf_op | source)
XLA Modules:
  0.0 534.6 jit_solution(1015549464468680743)
XLA Ops:
  11.3 3.6 convolution_convert_fusion.3
  16.1 33.9 %shard_map.174 = (bf16[8,32,2560]{2,1,0:T(8,128)(2,1)}, f32[8,8,128]{2,1,0:T(8,128)}) custom-call(bf16[8,32,2560]{2,1,0:T(8,128)(2,1)} %pad_maximum_fusion.refs_0_, f32[8,128]{1,0:T(8,128)} %pad.12.refs_1_), custom_call_target="tpu_custom_call" | custom-call | tf_op jit(solution)/shard_map/pallas_call | solution.py:109
  56.4 26.6 %shard_map.175 = bf16[8,32,2048]{2,1,0:T(8,128)(2,1)} custom-call(bf16[32,2048]{1,0:T(8,128)(2,1)} %bitcast.173), custom_call_target="tpu_custom_call" | custom-call | tf_op jit(solution)/shard_map/pallas_call | solution.py:109
  86.3 3.5 fusion.64
  91.0 3.0 fusion.30
  94.1 35.6 %shard_map.176 = (bf16[8,2,256,128]{3,2,1,0:T(8,128)(2,1)S(1)}, f32[8,2,256,128]{3,2,1,0:T(8,128)S(1)}) custom-call(s32[8]{0:T(128)S(1)} %subtract_clamp_fusion.length_ref, bf16[8,2,256,128]{3,2,1,0:T(8,128)(2,1)S(1)} %bitcast.150, bf16[8,2,4096,256]{3,2,1,0:T(8,128)(2,1)} %cache_ref.1), custom_call_target="tpu_custom_call" | custom-call | flops 8589934592 | bytes 33554432 | tf_op jit(solution)/shard_map/pallas_call | solution.py:163
  131.2 2.7 convolution_convert_fusion.1
  142.9 28.6 %shard_map.177 = (bf16[8,32,2048]{2,1,0:T(8,128)(2,1)}, f32[8,32,128]{2,1,0:T(8,128)}) custom-call(bf16[8,32,2048]{2,1,0:T(8,128)(2,1)} %bitcast.159, f32[8,32,128]{2,1,0:T(8,128)} %bitcast.172), custom_call_target="tpu_custom_call" | custom-call | tf_op jit(solution)/shard_map/pallas_call | solution.py:109
  182.1 27.2 %shard_map.178 = (bf16[8,32,2048]{2,1,0:T(8,128)(2,1)}, f32[8,16,128]{2,1,0:T(8,128)}) custom-call(bf16[32,2048]{1,0:T(8,128)(2,1)} %fusion.42.refs_0_, f32[16,128]{1,0:T(8,128)} %pad.14.refs_1_), custom_call_target="tpu_custom_call" | custom-call | tf_op jit(solution)/shard_map/pallas_call | solution.py:109
  209.4 4.8 fusion.4.refs_0_
  214.2 13.7 %shard_map.179 = f32[4,64,1024]{2,1,0:T(8,128)} custom-call(f32[4,64,1024]{2,1,0:T(8,128)} %fusion.4.refs_0_), custom_call_target="tpu_custom_call" | custom-call | tf_op jit(solution)/shard_map/pallas_call | solution.py:109
  231.5 27.4 %shard_map.180.refs_0_ = bf16[8,64,1024]{2,1,0:T(8,128)(2,1)} custom-call(bf16[64,1024]{1,0:T(8,128)(2,1)} %add_convert_fusion.1.refs_0_), custom_call_target="tpu_custom_call" | custom-call | tf_op jit(solution)/shard_map/pallas_call | solution.py:109
  258.9 33.0 %shard_map.181.refs_0_ = bf16[2,8,64,1024]{3,2,1,0:T(8,128)(2,1)} custom-call(bf16[8,64,1024]{2,1,0:T(8,128)(2,1)} %shard_map.180.refs_0_), custom_call_target="tpu_custom_call" | custom-call | tf_op jit(solution)/shard_map/pallas_call | solution.py:109
  291.8 64.9 %shard_map.182 = bf16[2,2,8,64,1024]{4,3,2,1,0:T(8,128)(2,1)} custom-call(bf16[2,8,64,1024]{3,2,1,0:T(8,128)(2,1)} %shard_map.181.refs_0_), custom_call_target="tpu_custom_call" | custom-call | tf_op jit(solution)/shard_map/pallas_call | solution.py:109
  356.8 3.1 multiply_reduce_fusion
  360.0 4.5 copy.200
  364.5 4.4 copy.225
  369.0 9.8 %fusion.20 = f32[256,896]{1,0:T(8,128)S(1)} fusion(bf16[8192,896]{1,0:T(8,128)(2,1)} %param.22, bf16[256,8192]{1,0:T(8,128)(2,1)S(1)} %bitcast.155, f32[8192]{0:T(1024)S(1)} %convert_element_type.108, f32[256]{0:T(256)S(1)} %rsqrt.19), kind=kOutput, calls=%fused_computation.23 | convolution fusion | flops 3764617216 | bytes 19825664 | tf_op jit(solution)/shard_map/dot_general | solution.py:372
  378.9 4.6 fusion.23
  383.5 10.1 %convolution_convert_fusion = bf16[256,8192]{1,0:T(8,128)(2,1)S(1)} fusion(bf16[256,896]{1,0:T(8,128)(2,1)S(1)} %fusion.23, bf16[896,8192]{1,0:T(8,128)(2,1)} %param.24), kind=kOutput, calls=%fused_computation | convolution fusion | flops 3760193536 | bytes 19333120 | tf_op jit(solution)/shard_map/dot_general | solution.py:382
  395.8 65.0 %shard_map.183 = bf16[2,128,8192]{2,1,0:T(8,128)(2,1)} custom-call(bf16[2,128,8192]{2,1,0:T(8,128)(2,1)} %bitcast.153), custom_call_target="tpu_custom_call" | custom-call | tf_op jit(solution)/shard_map/pallas_call | solution.py:109
  460.8 5.1 reduce_sum.149
  465.8 34.9 %shard_map.184 = bf16[2,64,8192]{2,1,0:T(8,128)(2,1)} custom-call(bf16[2,64,8192]{2,1,0:T(8,128)(2,1)} %bitcast.154), custom_call_target="tpu_custom_call" | custom-call | tf_op jit(solution)/shard_map/pallas_call | solution.py:109
  504.2 26.9 %shard_map.185 = bf16[8,64,1024]{2,1,0:T(8,128)(2,1)} custom-call(bf16[8,64,1024]{2,1,0:T(8,128)(2,1)} %reshape.353.refs_0_), custom_call_target="tpu_custom_call" | custom-call | tf_op jit(solution)/shard_map/pallas_call | solution.py:109
  (126 shorter events, 56.1 us)
Async XLA Ops:
  0.6 7.8 %copy-start = (bf16[1024,256]{1,0:T(8,128)(2,1)S(1)}, bf16[1024,256]{1,0:T(8,128)(2,1)}, u32[]{:S(2)}) copy-start(bf16[1024,256]{1,0:T(8,128)(2,1)} %param.19) | copy-start | bytes 1572868
  55.4 29.8 %copy-start.3 = (bf16[256,1024]{1,0:T(8,128)(2,1)S(1)}, bf16[256,1024]{1,0:T(8,128)(2,1)}, u32[]{:S(2)}) copy-start(bf16[256,1024]{1,0:T(8,128)(2,1)} %param.15) | copy-start | bytes 1572868
  171.5 8.5 %copy-start.4 = (bf16[8,32,2048]{2,1,0:T(8,128)(2,1)S(1)}, bf16[8,32,2048]{2,1,0:T(8,128)(2,1)}, u32[]{:S(2)}) copy-start(bf16[8,32,2048]{2,1,0:T(8,128)(2,1)} %get-tuple-element.17) | copy-start | bytes 3145732
  209.3 21.5 %copy-start.5 = (f32[8,16,128]{2,1,0:T(8,128)S(1)}, f32[8,16,128]{2,1,0:T(8,128)}, u32[]{:S(2)}) copy-start(f32[8,16,128]{2,1,0:T(8,128)} %get-tuple-element.19) | copy-start | bytes 196612
  364.5 14.3 %slice-start = ((s8[14680064]{0:T(1024)(128)(4,1)}), s8[4194304]{0:T(1024)(128)(4,1)S(1)}, s32[]{:S(2)}) async-start(s8[14680064]{0:T(1024)(128)(4,1)} %bitcast.185), calls=%async_computation | async-start | bytes 8388608
  368.9 9.9 %copy-start.2 = (bf16[32,8,8,1024]{3,1,2,0:T(8,128)(2,1)}, bf16[32,8,8,1024]{3,1,2,0:T(8,128)(2,1)S(1)}, u32[]{:S(2)}) copy-start(bf16[32,8,8,1024]{3,1,2,0:T(8,128)(2,1)S(1)} %copy.225) | copy-start | bytes 12582916
  368.9 9.9 %slice-start.1 = ((s8[14680064]{0:T(1024)(128)(4,1)}), s8[4194304]{0:T(1024)(128)(4,1)S(1)}, s32[]{:S(2)}) async-start(s8[14680064]{0:T(1024)(128)(4,1)} %bitcast.185), calls=%async_computation.1 | async-start | bytes 8388608
  369.0 9.9 %slice-start.2 = ((s8[14680064]{0:T(1024)(128)(4,1)}), s8[4194304]{0:T(1024)(128)(4,1)S(1)}, s32[]{:S(2)}) async-start(s8[14680064]{0:T(1024)(128)(4,1)} %bitcast.185), calls=%async_computation.2 | async-start | bytes 8388608
  369.0 9.9 %slice-start.3 = ((s8[14680064]{0:T(1024)(128)(4,1)}), s8[2097152]{0:T(1024)(128)(4,1)S(1)}, s32[]{:S(2)}) async-start(s8[14680064]{0:T(1024)(128)(4,1)} %bitcast.185), calls=%async_computation.3 | async-start | bytes 4194304
  465.8 68.4 %copy-start.1 = (bf16[1024,256]{1,0:T(8,128)(2,1)S(1)}, bf16[1024,256]{1,0:T(8,128)(2,1)}, u32[]{:S(2)}) copy-start(bf16[1024,256]{1,0:T(8,128)(2,1)} %param.19) | copy-start | bytes 1572868

commit v2 on v1

--- a/solution.py
+++ b/solution.py
@@ -64,7 +64,7 @@
     return (highest, jnp.sum(weights, axis=-1), weights.astype(jnp.bfloat16))
 
 
-def exchange_kernel(kinds, axis, stride, count, *refs):
+def exchange_kernel(kinds, axis, stride, count, cuts, *refs):
     total = len(kinds)
     sources, targets = refs[:total], refs[total : 2 * total]
     send_sem, recv_sem, own_sem = refs[2 * total :]
@@ -81,16 +81,19 @@
         other = lax.rem(place + step, count)
         peer = base + other * stride
         for a in range(total):
-            copy = pltpu.make_async_remote_copy(
-                src_ref=sources[a].at[other] if kinds[a] == "scatter" else sources[a],
-                dst_ref=targets[a].at[place],
-                send_sem=send_sem.at[a, step],
-                recv_sem=recv_sem.at[a, step],
-                device_id={axis: peer},
-                device_id_type=MESH,
-            )
-            copy.start()
-            copies.append(copy)
+            span = targets[a].shape[1] // cuts
+            for cut in range(cuts):
+                part = pl.ds(cut * span, span)
+                copy = pltpu.make_async_remote_copy(
+                    src_ref=sources[a].at[other, part] if kinds[a] == "scatter" else sources[a].at[part],
+                    dst_ref=targets[a].at[place, part],
+                    send_sem=send_sem.at[a, step, cut],
+                    recv_sem=recv_sem.at[a, step, cut],
+                    device_id={axis: peer},
+                    device_id_type=MESH,
+                )
+                copy.start()
+                copies.append(copy)
     own = []
     for a in range(total):
         copy = pltpu.make_async_copy(
@@ -104,10 +107,10 @@
         copy.wait()
 
 
-def exchange(arrays, kinds, axis, stride, count, identity):
+def exchange(arrays, kinds, axis, stride, count, identity, cuts=1):
     total = len(arrays)
     return pl.pallas_call(
-        functools.partial(exchange_kernel, kinds, axis, stride, count),
+        functools.partial(exchange_kernel, kinds, axis, stride, count, cuts),
         out_shape=[
             jax.ShapeDtypeStruct(a.shape if k == "scatter" else (count,) + a.shape, a.dtype)
             for a, k in zip(arrays, kinds)
@@ -115,8 +118,8 @@
         in_specs=[pl.BlockSpec(memory_space=pl.ANY)] * total,
         out_specs=[pl.BlockSpec(memory_space=pl.ANY)] * total,
         scratch_shapes=[
-            pltpu.SemaphoreType.DMA((total, count)),
-            pltpu.SemaphoreType.DMA((total, count)),
+            pltpu.SemaphoreType.DMA((total, count, cuts)),
+            pltpu.SemaphoreType.DMA((total, count, cuts)),
             pltpu.SemaphoreType.DMA((total,)),
         ],
         compiler_params=pltpu.CompilerParams(collective_id=identity, has_side_effects=True),
@@ -225,13 +228,18 @@
     own_rows = row_total // model_count
     head_width = head_local * HD
     kv_width = kv_local * HD
-    parts = jnp.concatenate([query_part, key_part, value_part], axis=1).astype(jnp.bfloat16)
+    entry_part = jnp.concatenate([key_part, value_part], axis=1)
     square_lanes = jnp.pad(square_part.reshape(row_total // HD, HD), ((0, 8 - row_total // HD), (0, 0)))
-    part_all, square_all = exchange(
-        [parts.reshape(model_count, own_rows, -1), square_lanes],
-        ("scatter", "gather"), "mp", 1, model_count, 1,
-    )
-    sums = jnp.sum(part_all.astype(jnp.float32), axis=0)
+    part_all, entry_all, square_all = exchange(
+        [
+            query_part.astype(jnp.bfloat16).reshape(model_count, own_rows, -1),
+            entry_part.reshape(model_count, own_rows, -1),
+            square_lanes,
+        ],
+        ("scatter", "scatter", "gather"), "mp", 1, model_count, 1,
+    )
+    query_sum = jnp.sum(part_all.astype(jnp.float32), axis=0)
+    entry_sum = jnp.sum(entry_all, axis=0)
     square_sum = jnp.sum(square_all, axis=0)[: row_total // HD].reshape(row_total)
     input_rms = jnp.sqrt(square_sum / D)
     inverse_rms = lax.rsqrt(square_sum / D + EPS)
@@ -243,14 +251,16 @@
     ).reshape(row_total)
     own_position = lax.dynamic_slice_in_dim(position, row_first, own_rows, 0)
     cosine, sine_table = rope_table(own_position, HD)
-    sums = sums * lax.dynamic_slice_in_dim(inverse_rms, row_first, own_rows, 0)[:, None]
+    own_inverse = lax.dynamic_slice_in_dim(inverse_rms, row_first, own_rows, 0)[:, None]
+    query_sum = query_sum * own_inverse
+    entry_sum = entry_sum * own_inverse
     query_rows = apply_rope(
-        sums[:, :head_width].reshape(own_rows, head_local, HD), cosine, sine_table
+        query_sum.reshape(own_rows, head_local, HD), cosine, sine_table
     ).astype(jnp.bfloat16)
     own_keys = apply_rope(
-        sums[:, head_width : head_width + kv_width].reshape(own_rows, kv_local, HD), cosine, sine_table
+        entry_sum[:, :kv_width].reshape(own_rows, kv_local, HD), cosine, sine_table
     ).astype(jnp.bfloat16)
-    own_values = sums[:, head_width + kv_width :].astype(jnp.bfloat16).reshape(own_rows, kv_local, HD)
+    own_values = entry_sum[:, kv_width:].astype(jnp.bfloat16).reshape(own_rows, kv_local, HD)
     entries = jnp.concatenate([own_keys, own_values], axis=-1).reshape(
         req_local, 2, kv_local, 2 * HD
     )
@@ -356,16 +366,14 @@
     head_part = jnp.dot(attention, w_out, preferred_element_type=jnp.float32)
     own_row = (model_index * seq_count + seq_index) * row_share
     seq_rows = row_total // seq_count
-    cores, chips = 2, seq_count // 2
     (head_all,) = exchange(
         [head_part.reshape(seq_count, seq_rows, -1)], ("scatter",), "seq", 1, seq_count, 5
     )
     wide_rows = lax.dynamic_slice_in_dim(wide_in, seq_index * seq_rows, seq_rows, 0)
     residual = (wide_rows + jnp.sum(head_all, axis=0)).astype(jnp.bfloat16)
     (piece_model,) = exchange([residual], ("gather",), "mp", 1, model_count, 6)
-    (piece_chip,) = exchange([piece_model], ("gather",), "seq", cores, chips, 7)
-    (piece_core,) = exchange([piece_chip], ("gather",), "seq", 1, cores, 8)
-    piece = jnp.transpose(piece_core, (1, 0, 3, 2, 4)).reshape(row_total, -1)
+    (piece_all,) = exchange([piece_model], ("gather",), "seq", 1, seq_count, 7)
+    piece = jnp.transpose(piece_all, (0, 2, 1, 3)).reshape(row_total, -1)
     wide_piece = piece.astype(jnp.float32)
     gain_piece = mlp_gain.astype(jnp.float32)
     scaled_piece = (wide_piece * gain_piece[None, :]).astype(jnp.bfloat16)
@@ -380,17 +388,11 @@
     up_value = up_acc * inverse_mid[:, None]
     hidden = (jax.nn.silu(gate_value) * up_value).astype(jnp.bfloat16)
     down = jnp.dot(hidden, w_down, preferred_element_type=jnp.float32).astype(jnp.bfloat16)
-    down = jnp.transpose(
-        down.reshape(model_count, chips, cores, row_share, D), (2, 1, 0, 3, 4)
-    )
-    (down_core,) = exchange(
-        [down.reshape(cores, chips * model_count * row_share, D)], ("scatter",), "seq", 1, cores, 9
-    )
-    down = jnp.sum(down_core.astype(jnp.float32), axis=0).astype(jnp.bfloat16)
-    (down_chip,) = exchange(
-        [down.reshape(chips, model_count * row_share, D)], ("scatter",), "seq", cores, chips, 10
-    )
-    down = jnp.sum(down_chip.astype(jnp.float32), axis=0).astype(jnp.bfloat16)
+    down = jnp.transpose(down.reshape(model_count, seq_count, row_share, D), (1, 0, 2, 3))
+    (down_seq,) = exchange(
+        [down.reshape(seq_count, model_count * row_share, D)], ("scatter",), "seq", 1, seq_count, 9
+    )
+    down = jnp.sum(down_seq.astype(jnp.float32), axis=0).astype(jnp.bfloat16)
     (down_model,) = exchange(
         [down.reshape(model_count, row_share * 8, D // 8)], ("scatter",), "mp", 1, model_count, 11
     )

time: 541 us -> 437 us (0.81)
  the two profiles are of different devices: /device:TPU:10 before, /device:TPU:0 now
where the time goes in v2:
time: 437 us; the launch traced here: 431 us
  Pallas kernels  316 us (72%)
  matrix products  48.8 us (11%)
  local copies, waits for them, and re-layouts  35.8 us (8%)
  other arithmetic  29.4 us (7%)
    pallas_call x9, Pallas kernels, exchange(): pl.pallas_call(functools.partial(exchange_kernel, kinds, axis, stride, co...  280 us
    pallas_call x1, Pallas kernels, prompt_terms(): pl.pallas_call(functools.partial(prompt_kernel, piece), out_shape=[jax.Sh...  35.6 us
    dot_general x1, matrix products, shards(): jnp.dot(hidden, w_down, preferred_element_type=jnp.float32)  9.93 us
    dot_general x1, matrix products, shards(): gate_acc = jnp.dot(scaled_piece, w_gate, preferred_element_type=jnp.float32)  9.83 us

profile of v2, /device:TPU:0, one launch (start us, length us, event | category | flops | bytes accessed | tf_op | source)
XLA Modules:
  0.0 431.2 jit_solution(13846403480635958767)
XLA Ops:
  13.1 4.4 %convolution_convert_fusion.3 = bf16[256,2048]{1,0:T(8,128)(2,1)} fusion(bf16[1024,2048]{1,0:T(8,128)(2,1)} %param.18, f32[1024]{0:T(1024)S(1)} %convert_element_type.92, bf16[256,1024]{1,0:T(8,128)(2,1)S(1)} %copy-done.2), kind=kOutput, calls=%fused_computation.16 | convolution fusion | flops 1075052544 | bytes 5771264 | tf_op jit(solution)/shard_map/dot_general | solution.py:224
  17.5 32.5 %shard_map.174 = (bf16[8,32,2048]{2,1,0:T(8,128)(2,1)}, f32[8,32,512]{2,1,0:T(8,128)}, f32[8,8,128]{2,1,0:T(8,128)}) custom-call(bf16[8,32,2048]{2,1,0:T(8,128)(2,1)} %bitcast.167, f32[8,32,512]{2,1,0:T(8,128)} %bitcast.161, f32[8,128]{1,0:T(8,128)} %pad.12.refs_2_), custom_call_target="tpu_custom_call" | custom-call | tf_op jit(solution)/shard_map/pallas_call | solution.py:112
  57.5 29.4 %shard_map.175 = bf16[8,32,2048]{2,1,0:T(8,128)(2,1)} custom-call(bf16[32,2048]{1,0:T(8,128)(2,1)} %bitcast.173), custom_call_target="tpu_custom_call" | custom-call | tf_op jit(solution)/shard_map/pallas_call | solution.py:112
  90.1 3.5 fusion.66
  95.5 3.0 fusion.30
  98.5 35.6 %shard_map.176 = (bf16[8,2,256,128]{3,2,1,0:T(8,128)(2,1)S(1)}, f32[8,2,256,128]{3,2,1,0:T(8,128)S(1)}) custom-call(s32[8]{0:T(128)S(1)} %subtract_clamp_fusion.length_ref, bf16[8,2,256,128]{3,2,1,0:T(8,128)(2,1)S(1)} %bitcast.150, bf16[8,2,4096,256]{3,2,1,0:T(8,128)(2,1)} %cache_ref.1), custom_call_target="tpu_custom_call" | custom-call | flops 8589934592 | bytes 33554432 | tf_op jit(solution)/shard_map/pallas_call | solution.py:166
  135.6 2.7 convolution_convert_fusion.1
  138.4 2.7 fusion.65
  147.4 27.2 %shard_map.177 = (bf16[8,32,2048]{2,1,0:T(8,128)(2,1)}, f32[8,32,128]{2,1,0:T(8,128)}) custom-call(bf16[8,32,2048]{2,1,0:T(8,128)(2,1)} %bitcast.158, f32[8,32,128]{2,1,0:T(8,128)} %bitcast.172), custom_call_target="tpu_custom_call" | custom-call | tf_op jit(solution)/shard_map/pallas_call | solution.py:112
  185.3 27.5 %shard_map.178 = (bf16[8,32,2048]{2,1,0:T(8,128)(2,1)}, f32[8,16,128]{2,1,0:T(8,128)}) custom-call(bf16[32,2048]{1,0:T(8,128)(2,1)} %fusion.44.refs_0_, f32[16,128]{1,0:T(8,128)} %pad.14.refs_1_), custom_call_target="tpu_custom_call" | custom-call | tf_op jit(solution)/shard_map/pallas_call | solution.py:112
  212.8 4.8 %fusion.4.refs_0_ = f32[4,64,1024]{2,1,0:T(8,128)} fusion(bf16[4,64,2048]{2,1,0:T(8,128)(2,1)} %bitcast.185, bf16[2048,1024]{1,0:T(8,128)(2,1)} %param.21), kind=kOutput, calls=%fused_computation.7 | convolution fusion | flops 1073741824 | bytes 6291456 | tf_op jit(solution)/shard_map/dot_general | solution.py:366
  217.6 13.7 %shard_map.179 = f32[4,64,1024]{2,1,0:T(8,128)} custom-call(f32[4,64,1024]{2,1,0:T(8,128)} %fusion.4.refs_0_), custom_call_target="tpu_custom_call" | custom-call | tf_op jit(solution)/shard_map/pallas_call | solution.py:112
  235.0 28.5 %shard_map.180.refs_0_ = bf16[8,64,1024]{2,1,0:T(8,128)(2,1)} custom-call(bf16[64,1024]{1,0:T(8,128)(2,1)} %add_convert_fusion.1.refs_0_), custom_call_target="tpu_custom_call" | custom-call | tf_op jit(solution)/shard_map/pallas_call | solution.py:112
  263.4 46.3 %shard_map.181 = bf16[4,8,64,1024]{3,2,1,0:T(8,128)(2,1)} custom-call(bf16[8,64,1024]{2,1,0:T(8,128)(2,1)} %shard_map.180.refs_0_), custom_call_target="tpu_custom_call" | custom-call | tf_op jit(solution)/shard_map/pallas_call | solution.py:112
  309.8 3.1 multiply_reduce_fusion
  313.0 4.5 %copy.175 = bf16[4,64,8,1024]{3,2,1,0:T(8,128)(2,1)S(1)} copy(bf16[4,64,8,1024]{3,1,2,0:T(8,128)(2,1)} %bitcast.151) | data formatting | bytes 8388608 | tf_op jit(solution)/shard_map/transpose | solution.py:376
  317.5 4.4 %copy.199 = bf16[32,8,8,1024]{3,1,2,0:T(8,128)(2,1)S(1)} copy(bf16[32,8,8,1024]{3,2,1,0:T(8,128)(2,1)S(1)} %bitcast.152) | data formatting | bytes 8388608
  322.0 9.8 %fusion.20 = f32[256,896]{1,0:T(8,128)S(1)} fusion(bf16[8192,896]{1,0:T(8,128)(2,1)} %param.22, bf16[256,8192]{1,0:T(8,128)(2,1)S(1)} %bitcast.154, f32[8192]{0:T(1024)S(1)} %copy-done.9, f32[256]{0:T(256)S(1)} %rsqrt.19), kind=kOutput, calls=%fused_computation.24 | convolution fusion | flops 3764617216 | bytes 19825664 | tf_op jit(solution)/shard_map/dot_general | solution.py:380
  331.9 4.5 %fusion.23 = bf16[256,896]{1,0:T(8,128)(2,1)S(1)} fusion(bf16[8192,896]{1,0:T(8,128)(2,1)S(1)} %bitcast.184, bf16[256,8192]{1,0:T(8,128)(2,1)S(1)} %bitcast.155, f32[8192]{0:T(1024)S(1)} %copy-done.9, f32[256,896]{1,0:T(8,128)S(1)} %fusion.20, f32[256]{0:T(256)S(1)} %rsqrt.19), kind=kOutput, calls=%fused_computation.27 | convolution fusion | flops 3765993472 | bytes 20284416 | tf_op jit(solution)/shard_map/dot_general | solution.py:381
  336.4 9.9 %convolution_convert_fusion = bf16[256,8192]{1,0:T(8,128)(2,1)S(1)} fusion(bf16[256,896]{1,0:T(8,128)(2,1)S(1)} %fusion.23, bf16[896,8192]{1,0:T(8,128)(2,1)} %param.24), kind=kOutput, calls=%fused_computation | convolution fusion | flops 3760193536 | bytes 19333120 | tf_op jit(solution)/shard_map/dot_general | solution.py:390
  346.4 2.2 copy.220
  348.6 47.8 %shard_map.182 = bf16[4,64,8192]{2,1,0:T(8,128)(2,1)} custom-call(bf16[4,64,8192]{2,1,0:T(8,128)(2,1)} %bitcast.153), custom_call_target="tpu_custom_call" | custom-call | tf_op jit(solution)/shard_map/pallas_call | solution.py:112
  396.4 3.1 reduce_sum.150
  400.8 27.3 %shard_map.183 = bf16[8,64,1024]{2,1,0:T(8,128)(2,1)} custom-call(bf16[8,64,1024]{2,1,0:T(8,128)(2,1)} %reshape.353.refs_0_), custom_call_target="tpu_custom_call" | custom-call | tf_op jit(solution)/shard_map/pallas_call | solution.py:112
  (136 shorter events, 51.3 us)
Async XLA Ops:
  0.6 8.5 %copy-start = (bf16[1024,256]{1,0:T(8,128)(2,1)S(1)}, bf16[1024,256]{1,0:T(8,128)(2,1)}, u32[]{:S(2)}) copy-start(bf16[1024,256]{1,0:T(8,128)(2,1)} %param.19) | copy-start | bytes 1572868
  0.6 12.5 %copy-start.2 = (bf16[256,1024]{1,0:T(8,128)(2,1)S(1)}, bf16[256,1024]{1,0:T(8,128)(2,1)}, u32[]{:S(2)}) copy-start(bf16[256,1024]{1,0:T(8,128)(2,1)} %param.15) | copy-start | bytes 1572868
  2.1 54.1 %copy-start.10 = (pred[2,2]{1,0:T(4,128)(4,1)}, pred[2,2]{1,0:T(4,128)(4,1)S(1)}, u32[]{:S(2)}) copy-start(pred[2,2]{1,0:T(4,128)(4,1)S(1)} %iota_compare_fusion.7) | copy-start | bytes 16
  56.2 32.8 %copy-start.6 = (f32[16,2,2,8,2]{3,4,1,2,0:T(2,128)}, f32[16,2,2,8,2]{3,4,1,2,0:T(2,128)S(1)}, u32[]{:S(2)}) copy-start(f32[16,2,2,8,2]{3,4,1,2,0:T(2,128)S(1)} %get-tuple-element.62) | copy-start | bytes 12292
  89.0 6.2 %copy-start.7 = (f32[16,2,2,8,2]{3,4,1,2,0:T(2,128)S(1)}, f32[16,2,2,8,2]{3,4,1,2,0:T(2,128)}, u32[]{:S(2)}) copy-start(f32[16,2,2,8,2]{3,4,1,2,0:T(2,128)} %copy-done.6) | copy-start | bytes 12292
  89.0 6.2 %copy-start.11 = (pred[2,2]{1,0:T(4,128)(4,1)S(1)}, pred[2,2]{1,0:T(4,128)(4,1)}, u32[]{:S(2)}) copy-start(pred[2,2]{1,0:T(4,128)(4,1)} %copy-done.10) | copy-start | bytes 16
  141.1 36.4 %copy-start.8 = (f32[32,16]{1,0:T(8,128)S(1)}, f32[32,16]{1,0:T(8,128)}, u32[]{:S(2)}) copy-start(f32[32,16]{1,0:T(8,128)} %reduce_sum.144) | copy-start | bytes 6148
  174.6 8.5 %copy-start.4 = (bf16[8,32,2048]{2,1,0:T(8,128)(2,1)S(1)}, bf16[8,32,2048]{2,1,0:T(8,128)(2,1)}, u32[]{:S(2)}) copy-start(bf16[8,32,2048]{2,1,0:T(8,128)(2,1)} %get-tuple-element.19) | copy-start | bytes 3145732
  212.8 21.5 %copy-start.5 = (f32[8,16,128]{2,1,0:T(8,128)S(1)}, f32[8,16,128]{2,1,0:T(8,128)}, u32[]{:S(2)}) copy-start(f32[8,16,128]{2,1,0:T(8,128)} %get-tuple-element.21) | copy-start | bytes 196612
  317.5 4.4 %copy-start.9 = (f32[8192]{0:T(1024)S(1)}, f32[8192]{0:T(1024)}, u32[]{:S(2)}) copy-start(f32[8192]{0:T(1024)} %convert_element_type.108) | copy-start | bytes 98308
  317.5 14.3 %slice-start = ((s8[14680064]{0:T(1024)(128)(4,1)}), s8[4194304]{0:T(1024)(128)(4,1)S(1)}, s32[]{:S(2)}) async-start(s8[14680064]{0:T(1024)(128)(4,1)} %bitcast.183), calls=%async_computation | async-start | bytes 8388608
  321.9 9.9 %copy-start.3 = (bf16[32,8,8,1024]{3,1,2,0:T(8,128)(2,1)}, bf16[32,8,8,1024]{3,1,2,0:T(8,128)(2,1)S(1)}, u32[]{:S(2)}) copy-start(bf16[32,8,8,1024]{3,1,2,0:T(8,128)(2,1)S(1)} %copy.199) | copy-start | bytes 12582916
  322.0 9.9 %slice-start.1 = ((s8[14680064]{0:T(1024)(128)(4,1)}), s8[4194304]{0:T(1024)(128)(4,1)S(1)}, s32[]{:S(2)}) async-start(s8[14680064]{0:T(1024)(128)(4,1)} %bitcast.183), calls=%async_computation.1 | async-start | bytes 8388608
  322.0 9.9 %slice-start.2 = ((s8[14680064]{0:T(1024)(128)(4,1)}), s8[4194304]{0:T(1024)(128)(4,1)S(1)}, s32[]{:S(2)}) async-start(s8[14680064]{0:T(1024)(128)(4,1)} %bitcast.183), calls=%async_computation.2 | async-start | bytes 8388608
  322.0 9.9 %slice-start.3 = ((s8[14680064]{0:T(1024)(128)(4,1)}), s8[2097152]{0:T(1024)(128)(4,1)S(1)}, s32[]{:S(2)}) async-start(s8[14680064]{0:T(1024)(128)(4,1)} %bitcast.183), calls=%async_computation.3 | async-start | bytes 4194304
  396.4 34.8 %copy-start.1 = (bf16[1024,256]{1,0:T(8,128)(2,1)S(1)}, bf16[1024,256]{1,0:T(8,128)(2,1)}, u32[]{:S(2)}) copy-start(bf16[1024,256]{1,0:T(8,128)(2,1)} %param.19) | copy-start | bytes 1572868
